TPU v7x, 256 devices: a whole 4x4x8 slice. The times are simulated.
256 devices in a mesh: group: 16 (over x_hi, y, core), fsdp: 16 (over x_lo, z).
Axes of the slice: x: 4 (x_hi: 2, x_lo: 2; x = x_hi * 2 + x_lo), y: 4, z: 8, core: 2. Of those that a mesh axis runs over, the one named last changes fastest.
Arguments:
- activations: bfloat16 [65536, 384], P(('group', 'fsdp')), may hold values from -6 to 6
- cotangent: bfloat16 [65536, 14336], P(('group', 'fsdp')), may hold values from -0.09375 to 0.09375
- params: float32 [16, 384, 14336], P('group', 'fsdp'), may hold values from -6 to 6
- moment: float32 [16, 384, 14336], P('group', 'fsdp'), may hold values from -3 to 3
- step_index: int32 [], replicated, may hold values from 0 to 999
Outputs:
- new_params: float32 [16, 384, 14336], P('group', 'fsdp')
- new_moment: float32 [16, 384, 14336], P('group', 'fsdp')
All inputs are finite; a program needn't handle non-finite values.
Results may differ from a plain program's by a relative error of at most 0.0009.
Values may be sent and summed in bfloat16 or wider, within the bound.
A program may use at most 256 MiB of HBM per device.

v0:
```python
from functools import partial

import jax
import jax.numpy as jnp
from jax import lax
from jax.sharding import PartitionSpec as P

rate_step = 0.1
momentum_coef = 0.9


def partner(block, axis, stride):
    count = lax.axis_size(axis)
    route = []
    for low in range(count):
        high = low | 1 << stride
        if high != low and high < count:
            route += [(low, high), (high, low)]
    return lax.ppermute(block, axis, route)


def flip_half(position, value):
    return partner(value, "group", position)


def trade(flipper, value, which_bit, bit_count):
    branches = [partial(flipper, position) for position in range(bit_count)]
    return lax.switch(which_bit, branches, value)


def contract_rows(left, right):
    return lax.dot_general(
        left, right, (((0,), (0,)), ((), ())), preferred_element_type=jnp.float32
    )


def on_device(activations, cotangent, params, moment, step_index):
    bit_count = lax.axis_size("group").bit_length() - 1
    which_bit = step_index % bit_count
    grad = lax.psum_scatter(
        contract_rows(activations, cotangent), "fsdp", scatter_dimension=0, tiled=True
    )
    grad = grad[None]
    new_moment = momentum_coef * moment + grad
    half_step = params - rate_step * (grad + momentum_coef * new_moment)
    new_params = 0.5 * (half_step + trade(flip_half, half_step, which_bit, bit_count))
    return (new_params, new_moment)


def solution(mesh):
    in_specs = (
        P(("group", "fsdp"), None),
        P(("group", "fsdp"), None),
        P("group", "fsdp", None),
        P("group", "fsdp", None),
        P(),
    )
    out_specs = (P("group", "fsdp", None), P("group", "fsdp", None))
    return jax.shard_map(
        on_device, mesh=mesh, in_specs=in_specs, out_specs=out_specs, check_vma=False
    )
```

profile of v0, /device:TPU:1, one launch (start us, length us, event | category | flops | bytes accessed | tf_op | source)
XLA Modules:
  0.0 309.4 jit_solution(18255356309200994318)
XLA Ops:
  7.2 0.0 copy-start
  7.2 0.0 reduce-scatter.2.cloned.1.call-start
  7.2 0.9 copy-done
  8.1 13.5 %fusion.2 = f32[384,14336]{1,0:T(8,128)} fusion(bf16[256,384]{1,0:T(8,128)(2,1)S(1)} %copy-done, bf16[256,14336]{1,0:T(8,128)(2,1)} %param.10), kind=kOutput, calls=%fused_computation.5 | convolution fusion | flops 2818572288 | bytes 29556736 | tf_op jit(solution)/shard_map/dot_general | solution.py:32
  21.6 0.0 copy-start.1
  21.6 0.0 reduce-scatter.2.cloned.1.call-update
  22.3 241.8 %reduce-scatter.2.cloned.1.call-done = f32[24,14336]{1,0:T(8,128)} async-done(((f32[384,14336]{1,0:T(8,128)}), f32[24,14336]{1,0:T(8,128)}) %reduce-scatter.2.cloned.1.call-update) | async-done | bytes 1376272 | tf_op jit(solution)/shard_map/reduce_scatter | solution.py:40
  264.1 0.0 copy-done.1
  264.1 3.2 %fusion.1 = (f32[1,24,14336]{2,1,0:T(8,128)S(1)}, f32[1,24,14336]{2,1,0:T(8,128)}) fusion(f32[1,24,14336]{2,1,0:T(8,128)S(1)} %copy-done.1, f32[24,14336]{1,0:T(8,128)} %reduce-scatter.2.cloned.1.call-done, f32[1,24,14336]{2,1,0:T(8,128)} %param.12), kind=kLoop, calls=%fused_computation.3 | loop fusion | flops 2064384 | bytes 6881280 | tf_op jit(solution)/shard_map/sub | solution.py:45
  267.3 32.7 %conditional.1 = (f32[1,24,14336]{2,1,0:T(8,128)}) conditional(s32[]{:T(128)} %clamp.3, f32[1,24,14336]{2,1,0:T(8,128)S(1)} %get-tuple-element.11, f32[1,24,14336]{2,1,0:T(8,128)S(1)} %get-tuple-element.11, f32[1,24,14336]{2,1,0:T(8,128)S(1)} %get-tuple-element.11, f32[1,24,14336]{2,1,0:T(8,128)S(1)} %get-tuple-element.11), branch_computations={%region_1.2_spmd, %region_2.3_spmd, %region_3.4_spmd, %region_4.5_... | conditional | bytes 5505072 | solution.py:28
  267.3 2.7 collective-permute-start.2
  270.0 30.0 %collective-permute-done.2 = f32[1,24,14336]{2,1,0:T(8,128)} collective-permute-done((f32[1,24,14336]{2,1,0:T(8,128)S(1)}, f32[1,24,14336]{2,1,0:T(8,128)}, u32[]{:S(2)}, u32[]{:S(2)}) %collective-permute-start.2) | collective-permute-done | bytes 1376288 | tf_op jit(solution)/shard_map/cond/branch_2_fun/ppermute | solution.py:19
  300.0 2.6 add_multiply_fusion
Async XLA Ops:
  7.2 0.9 copy-start
  7.2 256.9 %reduce-scatter.2.cloned.1.call-start = ((), (), s32[]{:S(2)}) async-start(), calls=%async_computation.1 | async-start | bytes 23396352 | tf_op jit(solution)/shard_map/reduce_scatter | solution.py:40
  21.6 242.6 %copy-start.1 = (f32[1,24,14336]{2,1,0:T(8,128)S(1)}, f32[1,24,14336]{2,1,0:T(8,128)}, u32[]{:S(2)}) copy-start(f32[1,24,14336]{2,1,0:T(8,128)} %param.11) | copy-start | bytes 4128772
  267.3 32.7 %collective-permute-start.2 = (f32[1,24,14336]{2,1,0:T(8,128)S(1)}, f32[1,24,14336]{2,1,0:T(8,128)}, u32[]{:S(2)}, u32[]{:S(2)}) collective-permute-start(f32[1,24,14336]{2,1,0:T(8,128)S(1)} %param.2), channel_id=1, source_target_pairs={{0,64},{64,0},{16,80},{80,16},{32,96},{96,32},{48,112},{112,48},{1... | collective-permute-start | bytes 4128776 | tf_op jit(solution)/shard_map/cond/branch_2_fun/ppermute | solution.py:19
Sparse Core Ops, SparseCore 0:
  21.7 242.3 reduce-scatter.1
where the time goes:
time: 310 us; the launch traced here: 309 us
  waiting for transfers between devices  272 us (88%)
  between operations  14.8 us (5%)
  matrix products  13.5 us (4%)
  other arithmetic  5.71 us (2%)
    reduce_scatter x1, waiting for transfers between devices, on_device(): lax.psum_scatter(contract_rows(activations, cotangent), 'fsdp', scatter_d...  242 us
    ppermute x1, waiting for transfers between devices, partner(): return lax.ppermute(block, axis, route)  30 us
    dot_general x1, matrix products, contract_rows(): lax.dot_general(left, right, (((0,), (0,)), ((), ())), preferred_element_...  13.5 us
  transfers between devices with their start and end apart: 2, of which 2 were waited for; matrix products, arithmetic and copies ran while one was open for 0% of the time, Pallas kernels for 0%

commit v1 on v0

v1 whole, which is shorter than its diff:
```python
from functools import partial

import jax
import jax.numpy as jnp
from jax import lax
from jax.experimental import pallas as pl
from jax.experimental.pallas import tpu as pltpu
from jax.sharding import PartitionSpec as P

RATE = 0.1
MOMENTUM = 0.9

HID = 14336
TOK = 256
WROWS = 384
ROWS = 24
NZ_RING = 8
C = 512

CODE_LOW = 30.0
CODE_HIGH = 11.2
CODE_STEPS = 32766.0 / (CODE_LOW + CODE_HIGH)
CODE_TINY = 2.0**-30

MESH = pl.DeviceIdType.MESH
PAIR_SLOTS = (2, 3, 5, 6, 8, 9, 11, 12, 14, 15)
UNITS = 18
HOP_LAG = 1
FIN_LAG = 1
MATE_LAG = 1
AHEAD = 2


def encode(v):
    size = jnp.maximum(jnp.abs(v), CODE_TINY)
    level = jnp.log2(size) * CODE_STEPS + (CODE_LOW * CODE_STEPS + 0.5)
    return jnp.where(v < 0.0, -level, level).astype(jnp.int32).astype(jnp.int16)


def decode(q):
    level = q.astype(jnp.int32).astype(jnp.float32)
    sign = jnp.clip(level, -1.0, 1.0)
    return sign * jnp.exp2(jnp.abs(level) * (1.0 / CODE_STEPS) - CODE_LOW)


def fold(v):
    half = v.shape[1] // 2
    return jnp.concatenate([v[:, :half], v[:, half:]], axis=0)


def unfold(v):
    half = v.shape[0] // 2
    return jnp.concatenate([v[:half], v[half:]], axis=1)


def kernel(
    mate_bit,
    pair_slots,
    units,
    x_ref,
    g_ref,
    params_ref,
    moment_ref,
    new_params,
    new_moment,
    x_own,
    x_near,
    xt_own,
    xt_near,
    g_own,
    g_near,
    p_own,
    m_own,
    part,
    ring_out,
    ring_in,
    total,
    fin_out,
    fin_in,
    mate_out,
    mate_in,
    x_sem,
    g_sem,
    pm_sem,
    near_send,
    near_recv,
    ring_send,
    ring_recv,
    fin_send,
    fin_recv,
    mate_send,
    mate_recv,
):
    n_pair = len(pair_slots)
    n_flat = units - n_pair
    group = lax.axis_index("group")
    index = lax.axis_index("fsdp")
    z = index % NZ_RING
    side = index // NZ_RING
    near = (group, (1 - side) * NZ_RING + z)
    low = group // 2**mate_bit % 2
    mate = (group + (1 - 2 * low) * 2**mate_bit, index)

    def along(step):
        return (group, side * NZ_RING + (z + step + NZ_RING) % NZ_RING)

    def pair_number(u):
        return sum((u > t).astype(jnp.int32) for t in pair_slots)

    def is_pair(u):
        return sum((u == t).astype(jnp.int32) for t in pair_slots) == 1

    def flat_col(u):
        return pl.multiple_of((u - pair_number(u)) * C, C)

    def pair_col(which, j):
        return pl.multiple_of((n_flat + which * n_pair + j) * C, C)

    def load_g(u, col):
        return pltpu.make_async_copy(
            g_ref.at[:, pl.ds(col, C)], g_own.at[u], g_sem.at[u]
        )

    def own_col(u):
        pair = is_pair(u).astype(jnp.int32)
        j = pair_number(u)
        return pl.multiple_of(
            pair * (n_flat + side * n_pair + j) * C + (1 - pair) * (u - j) * C, C
        )

    load_x = pltpu.make_async_copy(x_ref, x_own, x_sem)
    load_x.start()

    @pl.loop(0, units)
    def _(u):
        load_g(u, own_col(u)).start()

    load_p = pltpu.make_async_copy(params_ref.at[0], p_own, pm_sem.at[0])
    load_m = pltpu.make_async_copy(moment_ref.at[0], m_own, pm_sem.at[1])
    load_p.start()
    load_m.start()

    barrier = pltpu.get_barrier_semaphore()
    for device in (along(1), along(-1), near, mate):
        pl.semaphore_signal(barrier, inc=1, device_id=device, device_id_type=MESH)
    pl.semaphore_wait(barrier, 4)

    send_x = pltpu.make_async_remote_copy(
        src_ref=x_ref,
        dst_ref=x_near,
        send_sem=near_send.at[n_pair],
        recv_sem=near_recv.at[n_pair],
        device_id=near,
        device_id_type=MESH,
    )
    send_x.start()

    def send_g(j):
        return pltpu.make_async_remote_copy(
            src_ref=g_ref.at[:, pl.ds(pair_col(1 - side, j), C)],
            dst_ref=g_near.at[j],
            send_sem=near_send.at[j],
            recv_sem=near_recv.at[j],
            device_id=near,
            device_id_type=MESH,
        )

    for j in range(AHEAD):
        send_g(j).start()

    load_x.wait()
    xt_own[...] = x_own[...].astype(jnp.float32).T.astype(jnp.bfloat16)

    def ring(u, k, step):
        return pltpu.make_async_remote_copy(
            src_ref=ring_out.at[u, k],
            dst_ref=ring_in.at[u, k],
            send_sem=ring_send.at[u, k],
            recv_sem=ring_recv.at[u, k],
            device_id=along(step),
            device_id_type=MESH,
        )

    def own_rows(u, where):
        first = pl.multiple_of(where * ROWS, 8)
        second = pl.multiple_of(NZ_RING * ROWS + where * ROWS, 8)
        return jnp.concatenate(
            [part[u, pl.ds(first, ROWS), :], part[u, pl.ds(second, ROWS), :]], axis=0
        )

    def turn(u):
        return 1 - 2 * (u % 2)

    def place(u, distance):
        return (z + turn(u) * distance + NZ_RING) % NZ_RING

    def start(u):
        pair = is_pair(u)
        j = pair_number(u)

        @pl.when(jnp.logical_not(pair))
        def _():
            load_g(u, own_col(u)).wait()
            part[u] = jnp.dot(
                xt_own[...], g_own[u], preferred_element_type=jnp.float32
            )

        @pl.when(pair)
        def _():
            load_g(u, own_col(u)).wait()

            @pl.when(j == 0)
            def _():
                send_x.wait_recv()
                xt_near[...] = x_near[...].astype(jnp.float32).T.astype(jnp.bfloat16)

            send_g(j).wait_recv()

            @pl.when(j + AHEAD < n_pair)
            def _():
                send_g(j + AHEAD).start()

            part[u] = jnp.dot(
                xt_own[...], g_own[u], preferred_element_type=jnp.float32
            ) + jnp.dot(xt_near[...], g_near[j], preferred_element_type=jnp.float32)

        ring_out[u, 0] = encode(own_rows(u, place(u, 4)))
        ring(u, 0, turn(u)).start()
        ring_out[u, 4] = encode(own_rows(u, place(u, -3)))
        ring(u, 4, -turn(u)).start()

    def hop(h, u):
        ring(u, h - 1, turn(u)).wait_recv()
        ring_out[u, h] = encode(decode(ring_in[u, h - 1]) + own_rows(u, place(u, 4 - h)))
        ring(u, h, turn(u)).start()
        if h < 3:
            ring(u, h + 3, -turn(u)).wait_recv()
            ring_out[u, h + 4] = encode(
                decode(ring_in[u, h + 3]) + own_rows(u, place(u, h - 3))
            )
            ring(u, h + 4, -turn(u)).start()

    def fin(u):
        return pltpu.make_async_remote_copy(
            src_ref=fin_out.at[u],
            dst_ref=fin_in.at[u],
            send_sem=fin_send.at[u],
            recv_sem=fin_recv.at[u],
            device_id=near,
            device_id_type=MESH,
        )

    def finish(u):
        ring(u, 6, -turn(u)).wait_recv()
        ring(u, 3, turn(u)).wait_recv()
        total[u] = decode(ring_in[u, 3]) + decode(ring_in[u, 6]) + own_rows(u, z)
        other = total[u, pl.ds(pl.multiple_of((1 - side) * ROWS, 8), ROWS), :]
        fin_out[u] = encode(fold(other))
        fin(u).start()

    def mate_flat(u):
        return pltpu.make_async_remote_copy(
            src_ref=mate_out.at[u, :, pl.ds(0, C // 2)],
            dst_ref=mate_in.at[u, :, pl.ds(0, C // 2)],
            send_sem=mate_send.at[u],
            recv_sem=mate_recv.at[u],
            device_id=mate,
            device_id_type=MESH,
        )

    def mate_pair(u):
        return pltpu.make_async_remote_copy(
            src_ref=mate_out.at[u],
            dst_ref=mate_in.at[u],
            send_sem=mate_send.at[u],
            recv_sem=mate_recv.at[u],
            device_id=mate,
            device_id_type=MESH,
        )

    def step(col, grad):
        columns = pl.ds(col, C)
        moved = MOMENTUM * m_own[:, columns] + grad
        half = p_own[:, columns] - RATE * (grad + MOMENTUM * moved)
        new_moment[0, :, columns] = moved
        new_params[0, :, columns] = half
        return half

    def update(u):
        @pl.when(u == 0)
        def _():
            load_p.wait()
            load_m.wait()

        fin(u).wait_recv()
        near_sum = unfold(decode(fin_in[u]))
        own_sum = total[u, pl.ds(pl.multiple_of(side * ROWS, 8), ROWS), :]
        pair = is_pair(u)
        j = pair_number(u)

        @pl.when(jnp.logical_not(pair))
        def _():
            half = step(flat_col(u), own_sum + near_sum)
            mate_out[u, :, : C // 2] = encode(fold(half))
            mate_flat(u).start()

        @pl.when(pair)
        def _():
            own_half = step(pair_col(side, j), own_sum)
            near_half = step(pair_col(1 - side, j), near_sum)
            mate_out[u] = encode(jnp.concatenate([own_half, near_half], axis=0))
            mate_pair(u).start()

    def average(u):
        pair = is_pair(u)
        j = pair_number(u)

        @pl.when(jnp.logical_not(pair))
        def _():
            mate_flat(u).wait_recv()
            columns = pl.ds(flat_col(u), C)
            got = unfold(decode(mate_in[u, :, : C // 2]))
            new_params[0, :, columns] = 0.5 * (new_params[0, :, columns] + got)

        @pl.when(pair)
        def _():
            mate_pair(u).wait_recv()
            got = decode(mate_in[u])
            columns = pl.ds(pair_col(side, j), C)
            new_params[0, :, columns] = 0.5 * (new_params[0, :, columns] + got[:ROWS])
            columns = pl.ds(pair_col(1 - side, j), C)
            new_params[0, :, columns] = 0.5 * (new_params[0, :, columns] + got[ROWS:])

    stages = [(HOP_LAG * h, partial(hop, h)) for h in (3, 2, 1)]
    stages += [(0, start), (4 * HOP_LAG, finish)]
    stages += [(4 * HOP_LAG + FIN_LAG, update)]
    last = 4 * HOP_LAG + FIN_LAG + MATE_LAG
    stages += [(last, average)]

    @pl.loop(0, units + last)
    def _(s):
        for lag, stage in stages:
            u = s - lag

            @pl.when(jnp.logical_and(u >= 0, u < units))
            def _():
                stage(u)

    send_x.wait_send()

    @pl.loop(0, n_pair)
    def _(j):
        send_g(j).wait_send()

    @pl.loop(0, units)
    def _(u):
        for k in range(4):
            ring(u, k, 1).wait_send()
        for k in range(4, 7):
            ring(u, k, -1).wait_send()
        fin(u).wait_send()

        @pl.when(is_pair(u))
        def _():
            mate_pair(u).wait_send()

        @pl.when(jnp.logical_not(is_pair(u)))
        def _():
            mate_flat(u).wait_send()


def run(mate_bit, pair_slots, units, activations, cotangent, params, moment):
    n_pair = len(pair_slots)
    any_ref = pl.BlockSpec(memory_space=pl.ANY)
    vmem_ref = pl.BlockSpec(memory_space=pltpu.VMEM)
    dma = pltpu.SemaphoreType.DMA
    bf16, f32, i16 = jnp.bfloat16, jnp.float32, jnp.int16
    out = jax.ShapeDtypeStruct((1, ROWS, HID), f32)
    return pl.pallas_call(
        partial(kernel, mate_bit, pair_slots, units),
        out_shape=(out, out),
        in_specs=[any_ref] * 4,
        out_specs=(vmem_ref, vmem_ref),
        scratch_shapes=[
            pltpu.VMEM((TOK, WROWS), bf16),
            pltpu.VMEM((TOK, WROWS), bf16),
            pltpu.VMEM((WROWS, TOK), bf16),
            pltpu.VMEM((WROWS, TOK), bf16),
            pltpu.VMEM((units, TOK, C), bf16),
            pltpu.VMEM((n_pair, TOK, C), bf16),
            pltpu.VMEM((ROWS, HID), f32),
            pltpu.VMEM((ROWS, HID), f32),
            pltpu.VMEM((units, WROWS, C), f32),
            pltpu.VMEM((units, 7, 2 * ROWS, C), i16),
            pltpu.VMEM((units, 7, 2 * ROWS, C), i16),
            pltpu.VMEM((units, 2 * ROWS, C), f32),
            pltpu.VMEM((units, 2 * ROWS, C // 2), i16),
            pltpu.VMEM((units, 2 * ROWS, C // 2), i16),
            pltpu.VMEM((units, 2 * ROWS, C), i16),
            pltpu.VMEM((units, 2 * ROWS, C), i16),
            dma,
            dma((units,)),
            dma((2,)),
            dma((n_pair + 1,)),
            dma((n_pair + 1,)),
            dma((units, 7)),
            dma((units, 7)),
            dma((units,)),
            dma((units,)),
            dma((units,)),
            dma((units,)),
        ],
        compiler_params=pltpu.CompilerParams(
            collective_id=mate_bit, has_side_effects=True, vmem_limit_bytes=60 << 20
        ),
        cost_estimate=pl.CostEstimate(
            flops=2 * TOK * WROWS * HID, bytes_accessed=13 << 20, transcendentals=0
        ),
    )(activations, cotangent, params, moment)


def on_device(activations, cotangent, params, moment, step_index):
    bits = lax.axis_size("group").bit_length() - 1
    branches = [partial(run, bit, PAIR_SLOTS, UNITS) for bit in range(bits)]
    return lax.switch(
        step_index % bits, branches, activations, cotangent, params, moment
    )


def solution(mesh):
    in_specs = (
        P(("group", "fsdp"), None),
        P(("group", "fsdp"), None),
        P("group", "fsdp", None),
        P("group", "fsdp", None),
        P(),
    )
    out_specs = (P("group", "fsdp", None), P("group", "fsdp", None))
    return jax.shard_map(
        on_device, mesh=mesh, in_specs=in_specs, out_specs=out_specs, check_vma=False
    )
```

time: 310 us -> 122 us (0.39)
  waiting for transfers between devices: 272 us -> 0 us
  Pallas kernels: 0 us -> 118 us
  matrix products: 13.5 us -> 0 us
  between operations: 14.8 us -> 1.3 us
  other arithmetic: 5.71 us -> 0 us
    reduce_scatter x1 -> x0, waiting for transfers between devices: 242 us -> none  [on_device(): lax.psum_scatter(contract_rows(activations, cotangent), 'fsdp', scatter_d...]
    pallas_call x0 -> x1, Pallas kernels: none -> 118 us  [run(): pl.pallas_call(partial(kernel, mate_bit, pair_slots, units), out_shape=(o...]
    ppermute x1 -> x0, waiting for transfers between devices: 30 us -> none  [partner(): return lax.ppermute(block, axis, route)]
    dot_general x1 -> x0, matrix products: 13.5 us -> none  [contract_rows(): lax.dot_general(left, right, (((0,), (0,)), ((), ())), preferred_element_...]
    sub x1 -> x0, other arithmetic: 3.16 us -> none  [on_device(): half_step = params - rate_step * (grad + momentum_coef * new_moment)]
  transfers between devices with their start and end apart: 2 -> 0, of which waited for: 2 -> 0; matrix products, arithmetic and copies ran while one was open for 0% -> 0% of each run, Pallas kernels for 0% -> 0%
where the time goes in v1:
time: 122 us
  Pallas kernels  118 us (97%)
  local copies, waits for them, and re-layouts  2.16 us (2%)
  between operations  1.3 us (1%)
    pallas_call x1, Pallas kernels, run(): pl.pallas_call(partial(kernel, mate_bit, pair_slots, units), out_shape=(o...  118 us

profile of v1, /device:TPU:1, one launch (start us, length us, event | category | flops | bytes accessed | tf_op | source)
XLA Modules:
  0.0 121.6 jit_solution(14098488141162279427)
XLA Ops:
  1.3 118.2 %conditional.1 = ((f32[1,24,14336]{2,1,0:T(8,128)S(1)}, f32[1,24,14336]{2,1,0:T(8,128)S(1)})) conditional(s32[]{:T(128)} %clamp.3, (bf16[256,384]{1,0:T(8,128)(2,1)}, bf16[256,14336]{1,0:T(8,128)(2,1)}, f32[1,24,14336]{2,1,0:T(8,128)}, f32[1,24,14336]{2,1,0:T(8,128)}) %tuple.19, (bf16[256,384]{1,0:T(8,128)(2,1)}, ...), branch_computations={%region_0.1_spmd, %region_1.2_spmd, %region_2.3_spmd, %region_3.4_... | conditional | flops 2818572288 | bytes 13631496 | solution.py:425
  1.3 118.1 %branch_0_fun.1 = (f32[1,24,14336]{2,1,0:T(8,128)S(1)}, f32[1,24,14336]{2,1,0:T(8,128)S(1)}) custom-call(bf16[256,384]{1,0:T(8,128)(2,1)} %get-tuple-element.32.x_ref, bf16[256,14336]{1,0:T(8,128)(2,1)} %get-tuple-element.33.g_ref, f32[1,24,14336]{2,1,0:T(8,128)} %get-tuple-element.34.params_ref, f32[1,24,14336]{2,1,0:T(8,128)} %get-tuple-element.35.moment_ref), custom_call_target="tpu_custom_call" | custom-call | flops 2818572288 | bytes 13631488 | tf_op jit(solution)/shard_map/cond/branch_0_fun/pallas_call | solution.py:379
  119.5 1.1 copy.26
  120.5 1.1 copy.27

commit v2 on v1

--- a/solution.py
+++ b/solution.py
@@ -23,12 +23,13 @@
 CODE_TINY = 2.0**-30
 
 MESH = pl.DeviceIdType.MESH
-PAIR_SLOTS = (2, 3, 5, 6, 8, 9, 11, 12, 14, 15)
-UNITS = 18
-HOP_LAG = 1
-FIN_LAG = 1
-MATE_LAG = 1
+PAIR_SLOTS = (6, 7, 9, 10, 12, 13, 15, 17, 18)
+UNITS = 28 - len(PAIR_SLOTS)
+LAGS = (2, 4, 7, 11, 14, 18)
+ORDER = (3, 1, 2, 0, 4, 5, 6)
+DRAIN_LAG = 1
 AHEAD = 2
+EARLY = 3
 
 
 def encode(v):
@@ -61,6 +62,8 @@
     g_ref,
     params_ref,
     moment_ref,
+    new_params_ref,
+    new_moment_ref,
     new_params,
     new_moment,
     x_own,
@@ -90,6 +93,7 @@
     fin_recv,
     mate_send,
     mate_recv,
+    out_sem,
 ):
     n_pair = len(pair_slots)
     n_flat = units - n_pair
@@ -128,6 +132,10 @@
             pair * (n_flat + side * n_pair + j) * C + (1 - pair) * (u - j) * C, C
         )
 
+    barrier = pltpu.get_barrier_semaphore()
+    for device in (along(1), along(-1), near, mate):
+        pl.semaphore_signal(barrier, inc=1, device_id=device, device_id_type=MESH)
+
     load_x = pltpu.make_async_copy(x_ref, x_own, x_sem)
     load_x.start()
 
@@ -139,11 +147,6 @@
     load_m = pltpu.make_async_copy(moment_ref.at[0], m_own, pm_sem.at[1])
     load_p.start()
     load_m.start()
-
-    barrier = pltpu.get_barrier_semaphore()
-    for device in (along(1), along(-1), near, mate):
-        pl.semaphore_signal(barrier, inc=1, device_id=device, device_id_type=MESH)
-    pl.semaphore_wait(barrier, 4)
 
     send_x = pltpu.make_async_remote_copy(
         src_ref=x_ref,
@@ -153,7 +156,6 @@
         device_id=near,
         device_id_type=MESH,
     )
-    send_x.start()
 
     def send_g(j):
         return pltpu.make_async_remote_copy(
@@ -165,12 +167,6 @@
             device_id_type=MESH,
         )
 
-    for j in range(AHEAD):
-        send_g(j).start()
-
-    load_x.wait()
-    xt_own[...] = x_own[...].astype(jnp.float32).T.astype(jnp.bfloat16)
-
     def ring(u, k, step):
         return pltpu.make_async_remote_copy(
             src_ref=ring_out.at[u, k],
@@ -194,40 +190,45 @@
     def place(u, distance):
         return (z + turn(u) * distance + NZ_RING) % NZ_RING
 
+    def form_flat(u):
+        load_g(u, own_col(u)).wait()
+        part[u] = jnp.dot(xt_own[...], g_own[u], preferred_element_type=jnp.float32)
+
+    def form_pair(u):
+        j = pair_number(u)
+        load_g(u, own_col(u)).wait()
+
+        @pl.when(j == 0)
+        def _():
+            send_x.wait_recv()
+            xt_near[...] = x_near[...].astype(jnp.float32).T.astype(jnp.bfloat16)
+
+        send_g(j).wait_recv()
+
+        @pl.when(j + AHEAD < n_pair)
+        def _():
+            send_g(j + AHEAD).start()
+
+        part[u] = jnp.dot(
+            xt_own[...], g_own[u], preferred_element_type=jnp.float32
+        ) + jnp.dot(xt_near[...], g_near[j], preferred_element_type=jnp.float32)
+
+    def first_codes(u):
+        ring_out[u, 0] = encode(own_rows(u, place(u, 4)))
+        ring_out[u, 4] = encode(own_rows(u, place(u, -3)))
+
+    def launch(u):
+        ring(u, 0, turn(u)).start()
+        ring(u, 4, -turn(u)).start()
+
     def start(u):
-        pair = is_pair(u)
-        j = pair_number(u)
-
-        @pl.when(jnp.logical_not(pair))
-        def _():
-            load_g(u, own_col(u)).wait()
-            part[u] = jnp.dot(
-                xt_own[...], g_own[u], preferred_element_type=jnp.float32
-            )
-
-        @pl.when(pair)
-        def _():
-            load_g(u, own_col(u)).wait()
-
-            @pl.when(j == 0)
-            def _():
-                send_x.wait_recv()
-                xt_near[...] = x_near[...].astype(jnp.float32).T.astype(jnp.bfloat16)
-
-            send_g(j).wait_recv()
-
-            @pl.when(j + AHEAD < n_pair)
-            def _():
-                send_g(j + AHEAD).start()
-
-            part[u] = jnp.dot(
-                xt_own[...], g_own[u], preferred_element_type=jnp.float32
-            ) + jnp.dot(xt_near[...], g_near[j], preferred_element_type=jnp.float32)
-
-        ring_out[u, 0] = encode(own_rows(u, place(u, 4)))
-        ring(u, 0, turn(u)).start()
-        ring_out[u, 4] = encode(own_rows(u, place(u, -3)))
-        ring(u, 4, -turn(u)).start()
+        @pl.when(u >= EARLY)
+        def _():
+            pair = is_pair(u)
+            pl.when(jnp.logical_not(pair))(lambda: form_flat(u))
+            pl.when(pair)(lambda: form_pair(u))
+            first_codes(u)
+            launch(u)
 
     def hop(h, u):
         ring(u, h - 1, turn(u)).wait_recv()
@@ -278,13 +279,35 @@
             device_id_type=MESH,
         )
 
-    def step(col, grad):
+    def out_moment(u, which, col):
+        columns = pl.ds(col, C)
+        return pltpu.make_async_copy(
+            new_moment.at[:, columns],
+            new_moment_ref.at[0, :, columns],
+            out_sem.at[u, which],
+        )
+
+    def out_params(u, which, col):
+        columns = pl.ds(col, C)
+        return pltpu.make_async_copy(
+            new_params.at[:, columns],
+            new_params_ref.at[0, :, columns],
+            out_sem.at[u, 2 + which],
+        )
+
+    def step(u, which, col, grad):
         columns = pl.ds(col, C)
         moved = MOMENTUM * m_own[:, columns] + grad
         half = p_own[:, columns] - RATE * (grad + MOMENTUM * moved)
-        new_moment[0, :, columns] = moved
-        new_params[0, :, columns] = half
+        new_moment[:, columns] = moved
+        new_params[:, columns] = half
+        out_moment(u, which, col).start()
         return half
+
+    def mix(u, which, col, got):
+        columns = pl.ds(col, C)
+        new_params[:, columns] = 0.5 * (new_params[:, columns] + got)
+        out_params(u, which, col).start()
 
     def update(u):
         @pl.when(u == 0)
@@ -300,14 +323,14 @@
 
         @pl.when(jnp.logical_not(pair))
         def _():
-            half = step(flat_col(u), own_sum + near_sum)
+            half = step(u, 0, flat_col(u), own_sum + near_sum)
             mate_out[u, :, : C // 2] = encode(fold(half))
             mate_flat(u).start()
 
         @pl.when(pair)
         def _():
-            own_half = step(pair_col(side, j), own_sum)
-            near_half = step(pair_col(1 - side, j), near_sum)
+            own_half = step(u, 0, pair_col(side, j), own_sum)
+            near_half = step(u, 1, pair_col(1 - side, j), near_sum)
             mate_out[u] = encode(jnp.concatenate([own_half, near_half], axis=0))
             mate_pair(u).start()
 
@@ -318,61 +341,77 @@
         @pl.when(jnp.logical_not(pair))
         def _():
             mate_flat(u).wait_recv()
-            columns = pl.ds(flat_col(u), C)
-            got = unfold(decode(mate_in[u, :, : C // 2]))
-            new_params[0, :, columns] = 0.5 * (new_params[0, :, columns] + got)
+            mix(u, 0, flat_col(u), unfold(decode(mate_in[u, :, : C // 2])))
 
         @pl.when(pair)
         def _():
             mate_pair(u).wait_recv()
             got = decode(mate_in[u])
-            columns = pl.ds(pair_col(side, j), C)
-            new_params[0, :, columns] = 0.5 * (new_params[0, :, columns] + got[:ROWS])
-            columns = pl.ds(pair_col(1 - side, j), C)
-            new_params[0, :, columns] = 0.5 * (new_params[0, :, columns] + got[ROWS:])
-
-    stages = [(HOP_LAG * h, partial(hop, h)) for h in (3, 2, 1)]
-    stages += [(0, start), (4 * HOP_LAG, finish)]
-    stages += [(4 * HOP_LAG + FIN_LAG, update)]
-    last = 4 * HOP_LAG + FIN_LAG + MATE_LAG
-    stages += [(last, average)]
-
-    @pl.loop(0, units + last)
-    def _(s):
-        for lag, stage in stages:
-            u = s - lag
-
-            @pl.when(jnp.logical_and(u >= 0, u < units))
-            def _():
-                stage(u)
-
-    send_x.wait_send()
-
-    @pl.loop(0, n_pair)
-    def _(j):
-        send_g(j).wait_send()
-
-    @pl.loop(0, units)
-    def _(u):
+            mix(u, 0, pair_col(side, j), got[:ROWS])
+            mix(u, 1, pair_col(1 - side, j), got[ROWS:])
+
+    def drain(u):
         for k in range(4):
             ring(u, k, 1).wait_send()
         for k in range(4, 7):
             ring(u, k, -1).wait_send()
         fin(u).wait_send()
-
-        @pl.when(is_pair(u))
-        def _():
+        pair = is_pair(u)
+        j = pair_number(u)
+
+        @pl.when(pair)
+        def _():
+            send_g(j).wait_send()
             mate_pair(u).wait_send()
-
-        @pl.when(jnp.logical_not(is_pair(u)))
+            for which, col in ((0, pair_col(side, j)), (1, pair_col(1 - side, j))):
+                out_moment(u, which, col).wait()
+                out_params(u, which, col).wait()
+
+        @pl.when(jnp.logical_not(pair))
         def _():
             mate_flat(u).wait_send()
+            out_moment(u, 0, flat_col(u)).wait()
+            out_params(u, 0, flat_col(u)).wait()
+
+    load_x.wait()
+    xt_own[...] = x_own[...].astype(jnp.float32).T.astype(jnp.bfloat16)
+
+    @pl.loop(0, EARLY)
+    def _(u):
+        form_flat(u)
+        first_codes(u)
+
+    pl.semaphore_wait(barrier, 4)
+    send_x.start()
+
+    @pl.loop(0, EARLY)
+    def _(u):
+        launch(u)
+
+    for j in range(AHEAD):
+        send_g(j).start()
+
+    actions = (start, partial(hop, 1), partial(hop, 2), partial(hop, 3))
+    actions += (finish, update, average)
+    lags = (0, *LAGS)
+    last = lags[-1]
+    stages = [(lags[k], actions[k]) for k in ORDER] + [(last + DRAIN_LAG, drain)]
+
+    @pl.loop(0, units + last + DRAIN_LAG)
+    def _(s):
+        for lag, stage in stages:
+            u = s - lag
+
+            @pl.when(jnp.logical_and(u >= 0, u < units))
+            def _():
+                stage(u)
+
+    send_x.wait_send()
 
 
 def run(mate_bit, pair_slots, units, activations, cotangent, params, moment):
     n_pair = len(pair_slots)
     any_ref = pl.BlockSpec(memory_space=pl.ANY)
-    vmem_ref = pl.BlockSpec(memory_space=pltpu.VMEM)
     dma = pltpu.SemaphoreType.DMA
     bf16, f32, i16 = jnp.bfloat16, jnp.float32, jnp.int16
     out = jax.ShapeDtypeStruct((1, ROWS, HID), f32)
@@ -380,8 +419,10 @@
         partial(kernel, mate_bit, pair_slots, units),
         out_shape=(out, out),
         in_specs=[any_ref] * 4,
-        out_specs=(vmem_ref, vmem_ref),
+        out_specs=(any_ref, any_ref),
         scratch_shapes=[
+            pltpu.VMEM((ROWS, HID), f32),
+            pltpu.VMEM((ROWS, HID), f32),
             pltpu.VMEM((TOK, WROWS), bf16),
             pltpu.VMEM((TOK, WROWS), bf16),
             pltpu.VMEM((WROWS, TOK), bf16),
@@ -409,6 +450,7 @@
             dma((units,)),
             dma((units,)),
             dma((units,)),
+            dma((units, 4)),
         ],
         compiler_params=pltpu.CompilerParams(
             collective_id=mate_bit, has_side_effects=True, vmem_limit_bytes=60 << 20

time: 122 us -> 96.6 us (0.79); the launches traced: 122 us -> 94.7 us
  Pallas kernels: 118 us -> 91 us
    pallas_call x1, Pallas kernels: 118 us -> 91 us  [run(): pl.pallas_call(partial(kernel, mate_bit, pair_slots, units), out_shape=(o...]
where the time goes in v2:
time: 96.6 us; the launch traced here: 94.7 us
  Pallas kernels  91 us (94%)
  local copies, waits for them, and re-layouts  2.16 us (2%)
  between operations  1.3 us (1%)
    pallas_call x1, Pallas kernels, run(): pl.pallas_call(partial(kernel, mate_bit, pair_slots, units), out_shape=(o...  91 us
    unnamed x2, local copies, waits for them, and re-layouts  2.16 us

profile of v2, /device:TPU:1, one launch (start us, length us, event | category | flops | bytes accessed | tf_op | source)
XLA Modules:
  0.0 94.7 jit_solution(173567712156817966)
XLA Ops:
  1.3 91.3 %conditional.1 = ((f32[1,24,14336]{2,1,0:T(8,128)S(1)}, f32[1,24,14336]{2,1,0:T(8,128)S(1)})) conditional(s32[]{:T(128)} %clamp.3, (bf16[256,384]{1,0:T(8,128)(2,1)}, bf16[256,14336]{1,0:T(8,128)(2,1)}, f32[1,24,14336]{2,1,0:T(8,128)}, f32[1,24,14336]{2,1,0:T(8,128)}) %tuple.19, (bf16[256,384]{1,0:T(8,128)(2,1)}, ...), branch_computations={%region_0.1_spmd, %region_1.2_spmd, %region_2.3_spmd, %region_3.4_... | conditional | flops 2818572288 | bytes 13631496 | solution.py:467
  1.3 91.0 %branch_1_fun.1 = (f32[1,24,14336]{2,1,0:T(8,128)S(1)}, f32[1,24,14336]{2,1,0:T(8,128)S(1)}) custom-call(bf16[256,384]{1,0:T(8,128)(2,1)} %get-tuple-element.36.x_ref, bf16[256,14336]{1,0:T(8,128)(2,1)} %get-tuple-element.37.g_ref, f32[1,24,14336]{2,1,0:T(8,128)} %get-tuple-element.38.params_ref, f32[1,24,14336]{2,1,0:T(8,128)} %get-tuple-element.39.moment_ref), custom_call_target="tpu_custom_call" | custom-call | flops 2818572288 | bytes 13631488 | tf_op jit(solution)/shard_map/cond/branch_1_fun/pallas_call | solution.py:418
  92.6 1.1 %copy.26 = f32[1,24,14336]{2,1,0:T(8,128)} copy(f32[1,24,14336]{2,1,0:T(8,128)S(1)} %get-tuple-element.70) | data formatting | bytes 2752512
  93.7 1.1 %copy.27 = f32[1,24,14336]{2,1,0:T(8,128)} copy(f32[1,24,14336]{2,1,0:T(8,128)S(1)} %get-tuple-element.71) | data formatting | bytes 2752512

commit v3 on v2

--- a/solution.py
+++ b/solution.py
@@ -25,9 +25,12 @@
 MESH = pl.DeviceIdType.MESH
 PAIR_SLOTS = (6, 7, 9, 10, 12, 13, 15, 17, 18)
 UNITS = 28 - len(PAIR_SLOTS)
-LAGS = (2, 4, 7, 11, 14, 18)
+LAGS = (2, 4, 7, 10, 13, 17)
 ORDER = (3, 1, 2, 0, 4, 5, 6)
 DRAIN_LAG = 1
+FIN_FROM = 0
+UPDATE_FROM = 0
+LATE = 1
 AHEAD = 2
 EARLY = 3
 
@@ -80,6 +83,7 @@
     total,
     fin_out,
     fin_in,
+    cross_in,
     mate_out,
     mate_in,
     x_sem,
@@ -91,6 +95,8 @@
     ring_recv,
     fin_send,
     fin_recv,
+    cross_send,
+    cross_recv,
     mate_send,
     mate_recv,
     out_sem,
@@ -104,6 +110,7 @@
     near = (group, (1 - side) * NZ_RING + z)
     low = group // 2**mate_bit % 2
     mate = (group + (1 - 2 * low) * 2**mate_bit, index)
+    cross = (mate[0], near[1])
 
     def along(step):
         return (group, side * NZ_RING + (z + step + NZ_RING) % NZ_RING)
@@ -133,7 +140,7 @@
         )
 
     barrier = pltpu.get_barrier_semaphore()
-    for device in (along(1), along(-1), near, mate):
+    for device in (along(1), along(-1), near, mate, cross):
         pl.semaphore_signal(barrier, inc=1, device_id=device, device_id_type=MESH)
 
     load_x = pltpu.make_async_copy(x_ref, x_own, x_sem)
@@ -257,7 +264,39 @@
         total[u] = decode(ring_in[u, 3]) + decode(ring_in[u, 6]) + own_rows(u, z)
         other = total[u, pl.ds(pl.multiple_of((1 - side) * ROWS, 8), ROWS), :]
         fin_out[u] = encode(fold(other))
+
+        @pl.when(u >= units - LATE)
+        def _():
+            crossing(u).start()
+            pair = is_pair(u)
+            j = pair_number(u)
+            own_sum = total[u, pl.ds(pl.multiple_of(side * ROWS, 8), ROWS), :]
+
+            @pl.when(jnp.logical_not(pair))
+            def _():
+                half = half_of(flat_col(u), own_sum)
+                mate_out[u, :, : C // 2] = encode(fold(half))
+                mate_flat(u).start()
+
+            @pl.when(pair)
+            def _():
+                own_half = half_of(pair_col(side, j), own_sum)
+                near_half = half_of(pair_col(1 - side, j), jnp.zeros_like(own_sum))
+                mate_out[u] = encode(jnp.concatenate([own_half, near_half], axis=0))
+                mate_pair(u).start()
+
+    def send_fin(u):
         fin(u).start()
+
+    def crossing(u):
+        return pltpu.make_async_remote_copy(
+            src_ref=fin_out.at[u],
+            dst_ref=cross_in.at[u - (units - LATE)],
+            send_sem=cross_send.at[u - (units - LATE)],
+            recv_sem=cross_recv.at[u - (units - LATE)],
+            device_id=cross,
+            device_id_type=MESH,
+        )
 
     def mate_flat(u):
         return pltpu.make_async_remote_copy(
@@ -295,6 +334,11 @@
             out_sem.at[u, 2 + which],
         )
 
+    def half_of(col, grad):
+        columns = pl.ds(col, C)
+        moved = MOMENTUM * m_own[:, columns] + grad
+        return p_own[:, columns] - RATE * (grad + MOMENTUM * moved)
+
     def step(u, which, col, grad):
         columns = pl.ds(col, C)
         moved = MOMENTUM * m_own[:, columns] + grad
@@ -320,14 +364,39 @@
         own_sum = total[u, pl.ds(pl.multiple_of(side * ROWS, 8), ROWS), :]
         pair = is_pair(u)
         j = pair_number(u)
-
-        @pl.when(jnp.logical_not(pair))
+        late = u >= units - LATE
+        soon = jnp.logical_not(late)
+
+        @pl.when(late)
+        def _():
+            crossing(u).wait_recv()
+            far = (RATE * (1.0 + MOMENTUM)) * unfold(
+                decode(cross_in[u - (units - LATE)])
+            )
+
+            @pl.when(jnp.logical_not(pair))
+            def _():
+                col = flat_col(u)
+                step(u, 0, col, own_sum + near_sum)
+                mate_flat(u).wait_recv()
+                mix(u, 0, col, unfold(decode(mate_in[u, :, : C // 2])) - far)
+
+            @pl.when(pair)
+            def _():
+                step(u, 0, pair_col(side, j), own_sum)
+                step(u, 1, pair_col(1 - side, j), near_sum)
+                mate_pair(u).wait_recv()
+                got = decode(mate_in[u])
+                mix(u, 0, pair_col(side, j), got[:ROWS])
+                mix(u, 1, pair_col(1 - side, j), got[ROWS:] - far)
+
+        @pl.when(jnp.logical_and(soon, jnp.logical_not(pair)))
         def _():
             half = step(u, 0, flat_col(u), own_sum + near_sum)
             mate_out[u, :, : C // 2] = encode(fold(half))
             mate_flat(u).start()
 
-        @pl.when(pair)
+        @pl.when(jnp.logical_and(soon, pair))
         def _():
             own_half = step(u, 0, pair_col(side, j), own_sum)
             near_half = step(u, 1, pair_col(1 - side, j), near_sum)
@@ -338,12 +407,14 @@
         pair = is_pair(u)
         j = pair_number(u)
 
-        @pl.when(jnp.logical_not(pair))
+        soon = u < units - LATE
+
+        @pl.when(jnp.logical_and(soon, jnp.logical_not(pair)))
         def _():
             mate_flat(u).wait_recv()
             mix(u, 0, flat_col(u), unfold(decode(mate_in[u, :, : C // 2])))
 
-        @pl.when(pair)
+        @pl.when(jnp.logical_and(soon, pair))
         def _():
             mate_pair(u).wait_recv()
             got = decode(mate_in[u])
@@ -356,6 +427,11 @@
         for k in range(4, 7):
             ring(u, k, -1).wait_send()
         fin(u).wait_send()
+
+        @pl.when(u >= units - LATE)
+        def _():
+            crossing(u).wait_send()
+
         pair = is_pair(u)
         j = pair_number(u)
 
@@ -381,7 +457,7 @@
         form_flat(u)
         first_codes(u)
 
-    pl.semaphore_wait(barrier, 4)
+    pl.semaphore_wait(barrier, 5)
     send_x.start()
 
     @pl.loop(0, EARLY)
@@ -395,16 +471,28 @@
     actions += (finish, update, average)
     lags = (0, *LAGS)
     last = lags[-1]
-    stages = [(lags[k], actions[k]) for k in ORDER] + [(last + DRAIN_LAG, drain)]
+
+    def done(k, s):
+        count = s + 1 - lags[k]
+        if k == 5:
+            count = jnp.minimum(count, 2 * (s + 1 - UPDATE_FROM))
+        return jnp.clip(count, 0, units)
+
+    def fins(s):
+        return jnp.where(s < FIN_FROM, 0, jnp.clip(s + 1 - lags[4], 0, units))
 
     @pl.loop(0, units + last + DRAIN_LAG)
     def _(s):
-        for lag, stage in stages:
-            u = s - lag
-
-            @pl.when(jnp.logical_and(u >= 0, u < units))
-            def _():
-                stage(u)
+        for k in ORDER:
+            if k == 5:
+                pl.loop(done(k, s - 1), done(k, s))(update)
+                continue
+            u = s - lags[k]
+            pl.when(jnp.logical_and(u >= 0, u < units))(partial(actions[k], u))
+            if k == 4:
+                pl.loop(fins(s - 1), fins(s))(send_fin)
+        u = s - last - DRAIN_LAG
+        pl.when(u >= 0)(partial(drain, u))
 
     send_x.wait_send()
 
@@ -437,6 +525,7 @@
             pltpu.VMEM((units, 2 * ROWS, C), f32),
             pltpu.VMEM((units, 2 * ROWS, C // 2), i16),
             pltpu.VMEM((units, 2 * ROWS, C // 2), i16),
+            pltpu.VMEM((LATE, 2 * ROWS, C // 2), i16),
             pltpu.VMEM((units, 2 * ROWS, C), i16),
             pltpu.VMEM((units, 2 * ROWS, C), i16),
             dma,
@@ -448,12 +537,14 @@
             dma((units, 7)),
             dma((units,)),
             dma((units,)),
+            dma((LATE,)),
+            dma((LATE,)),
             dma((units,)),
             dma((units,)),
             dma((units, 4)),
         ],
         compiler_params=pltpu.CompilerParams(
-            collective_id=mate_bit, has_side_effects=True, vmem_limit_bytes=60 << 20
+            collective_id=mate_bit, has_side_effects=True, vmem_limit_bytes=50 << 20
         ),
         cost_estimate=pl.CostEstimate(
             flops=2 * TOK * WROWS * HID, bytes_accessed=13 << 20, transcendentals=0

time: 96.6 us -> 97.5 us (level)
  Pallas kernels: 91 us -> 92.3 us
    pallas_call x1, Pallas kernels: 91 us -> 92.3 us  [run(): pl.pallas_call(partial(kernel, mate_bit, pair_slots, units), out_shape=(o...]
where the time goes in v3:
time: 97.5 us; the launch traced here: 96.2 us
  Pallas kernels  92.3 us (95%)
  local copies, waits for them, and re-layouts  2.16 us (2%)
  between operations  1.3 us (1%)
    pallas_call x1, Pallas kernels, run(): pl.pallas_call(partial(kernel, mate_bit, pair_slots, units), out_shape=(o...  92.3 us
    unnamed x2, local copies, waits for them, and re-layouts  2.16 us

profile of v3, /device:TPU:1, one launch (start us, length us, event | category | flops | bytes accessed | tf_op | source)
XLA Modules:
  0.0 96.2 jit_solution(4202491897214871129)
XLA Ops:
  1.3 92.7 %conditional.1 = ((f32[1,24,14336]{2,1,0:T(8,128)S(1)}, f32[1,24,14336]{2,1,0:T(8,128)S(1)})) conditional(s32[]{:T(128)} %clamp.3, (bf16[256,384]{1,0:T(8,128)(2,1)}, bf16[256,14336]{1,0:T(8,128)(2,1)}, f32[1,24,14336]{2,1,0:T(8,128)}, f32[1,24,14336]{2,1,0:T(8,128)}) %tuple.19, (bf16[256,384]{1,0:T(8,128)(2,1)}, ...), branch_computations={%region_0.1_spmd, %region_1.2_spmd, %region_2.3_spmd, %region_3.4_... | conditional | flops 2818572288 | bytes 13631496 | solution.py:558
  1.3 92.3 %branch_2_fun.1 = (f32[1,24,14336]{2,1,0:T(8,128)S(1)}, f32[1,24,14336]{2,1,0:T(8,128)S(1)}) custom-call(bf16[256,384]{1,0:T(8,128)(2,1)} %get-tuple-element.40.x_ref, bf16[256,14336]{1,0:T(8,128)(2,1)} %get-tuple-element.41.g_ref, f32[1,24,14336]{2,1,0:T(8,128)} %get-tuple-element.42.params_ref, f32[1,24,14336]{2,1,0:T(8,128)} %get-tuple-element.43.moment_ref), custom_call_target="tpu_custom_call" | custom-call | flops 2818572288 | bytes 13631488 | tf_op jit(solution)/shard_map/cond/branch_2_fun/pallas_call | solution.py:506
  94.0 1.1 %copy.26 = f32[1,24,14336]{2,1,0:T(8,128)} copy(f32[1,24,14336]{2,1,0:T(8,128)S(1)} %get-tuple-element.70) | data formatting | bytes 2752512
  95.1 1.1 %copy.27 = f32[1,24,14336]{2,1,0:T(8,128)} copy(f32[1,24,14336]{2,1,0:T(8,128)S(1)} %get-tuple-element.71) | data formatting | bytes 2752512

commit v4 on v3

--- a/solution.py
+++ b/solution.py
@@ -28,8 +28,6 @@
 LAGS = (2, 4, 7, 10, 13, 17)
 ORDER = (3, 1, 2, 0, 4, 5, 6)
 DRAIN_LAG = 1
-FIN_FROM = 0
-UPDATE_FROM = 0
 LATE = 1
 AHEAD = 2
 EARLY = 3
@@ -234,8 +232,10 @@
             pair = is_pair(u)
             pl.when(jnp.logical_not(pair))(lambda: form_flat(u))
             pl.when(pair)(lambda: form_pair(u))
-            first_codes(u)
-            launch(u)
+            ring_out[u, 0] = encode(own_rows(u, place(u, 4)))
+            ring(u, 0, turn(u)).start()
+            ring_out[u, 4] = encode(own_rows(u, place(u, -3)))
+            ring(u, 4, -turn(u)).start()
 
     def hop(h, u):
         ring(u, h - 1, turn(u)).wait_recv()
@@ -264,6 +264,7 @@
         total[u] = decode(ring_in[u, 3]) + decode(ring_in[u, 6]) + own_rows(u, z)
         other = total[u, pl.ds(pl.multiple_of((1 - side) * ROWS, 8), ROWS), :]
         fin_out[u] = encode(fold(other))
+        fin(u).start()
 
         @pl.when(u >= units - LATE)
         def _():
@@ -285,8 +286,6 @@
                 mate_out[u] = encode(jnp.concatenate([own_half, near_half], axis=0))
                 mate_pair(u).start()
 
-    def send_fin(u):
-        fin(u).start()
 
     def crossing(u):
         return pltpu.make_async_remote_copy(
@@ -472,25 +471,11 @@
     lags = (0, *LAGS)
     last = lags[-1]
 
-    def done(k, s):
-        count = s + 1 - lags[k]
-        if k == 5:
-            count = jnp.minimum(count, 2 * (s + 1 - UPDATE_FROM))
-        return jnp.clip(count, 0, units)
-
-    def fins(s):
-        return jnp.where(s < FIN_FROM, 0, jnp.clip(s + 1 - lags[4], 0, units))
-
     @pl.loop(0, units + last + DRAIN_LAG)
     def _(s):
         for k in ORDER:
-            if k == 5:
-                pl.loop(done(k, s - 1), done(k, s))(update)
-                continue
             u = s - lags[k]
             pl.when(jnp.logical_and(u >= 0, u < units))(partial(actions[k], u))
-            if k == 4:
-                pl.loop(fins(s - 1), fins(s))(send_fin)
         u = s - last - DRAIN_LAG
         pl.when(u >= 0)(partial(drain, u))
 

time: 97.5 us -> 95.7 us (0.982)
  Pallas kernels: 92.3 us -> 90.6 us
    pallas_call x1, Pallas kernels: 92.3 us -> 90.6 us  [run(): pl.pallas_call(partial(kernel, mate_bit, pair_slots, units), out_shape=(o...]
where the time goes in v4:
time: 95.7 us; the launch traced here: 94.3 us
  Pallas kernels  90.6 us (95%)
  local copies, waits for them, and re-layouts  2.16 us (2%)
  between operations  1.3 us (1%)
    pallas_call x1, Pallas kernels, run(): pl.pallas_call(partial(kernel, mate_bit, pair_slots, units), out_shape=(o...  90.6 us
    unnamed x2, local copies, waits for them, and re-layouts  2.16 us

profile of v4, /device:TPU:1, one launch (start us, length us, event | category | flops | bytes accessed | tf_op | source)
XLA Modules:
  0.0 94.3 jit_solution(11715739243053394355)
XLA Ops:
  1.3 90.8 %conditional.1 = ((f32[1,24,14336]{2,1,0:T(8,128)S(1)}, f32[1,24,14336]{2,1,0:T(8,128)S(1)})) conditional(s32[]{:T(128)} %clamp.3, (bf16[256,384]{1,0:T(8,128)(2,1)}, bf16[256,14336]{1,0:T(8,128)(2,1)}, f32[1,24,14336]{2,1,0:T(8,128)}, f32[1,24,14336]{2,1,0:T(8,128)}) %tuple.19, (bf16[256,384]{1,0:T(8,128)(2,1)}, ...), branch_computations={%region_0.1_spmd, %region_1.2_spmd, %region_2.3_spmd, %region_3.4_... | conditional | flops 2818572288 | bytes 13631496 | solution.py:543
  1.3 90.6 %branch_1_fun.1 = (f32[1,24,14336]{2,1,0:T(8,128)S(1)}, f32[1,24,14336]{2,1,0:T(8,128)S(1)}) custom-call(bf16[256,384]{1,0:T(8,128)(2,1)} %get-tuple-element.36.x_ref, bf16[256,14336]{1,0:T(8,128)(2,1)} %get-tuple-element.37.g_ref, f32[1,24,14336]{2,1,0:T(8,128)} %get-tuple-element.38.params_ref, f32[1,24,14336]{2,1,0:T(8,128)} %get-tuple-element.39.moment_ref), custom_call_target="tpu_custom_call" | custom-call | flops 2818572288 | bytes 13631488 | tf_op jit(solution)/shard_map/cond/branch_1_fun/pallas_call | solution.py:491
  92.1 1.1 %copy.26 = f32[1,24,14336]{2,1,0:T(8,128)} copy(f32[1,24,14336]{2,1,0:T(8,128)S(1)} %get-tuple-element.70) | data formatting | bytes 2752512
  93.2 1.1 %copy.27 = f32[1,24,14336]{2,1,0:T(8,128)} copy(f32[1,24,14336]{2,1,0:T(8,128)S(1)} %get-tuple-element.71) | data formatting | bytes 2752512
